TPU v7x, 32 devices: a whole 2x2x4 slice. The times are simulated.
32 devices in a mesh: dp: 4 (over y, x), expert: 8 (over z, core).
Axes of the slice: x: 2, y: 2, z: 4, core: 2. Of those that a mesh axis runs over, the one named last changes fastest.
Arguments:
- tokens: bfloat16 [73728, 512], P(('dp', 'expert')), may hold values from -6 to 6
- gain_one: float32 [512], replicated, may hold values from 0.1 to 1.9
- w_qkv: bfloat16 [512, 1536], replicated, may hold values from -0.25 to 0.25
- w_attn_out: bfloat16 [512, 512], replicated, may hold values from -1 to 1
- gain_two: float32 [512], replicated, may hold values from 0.1 to 1.9
- w_router: bfloat16 [512, 8], replicated, may hold values from -0.1875 to 0.1875
- w_first: bfloat16 [8, 512, 2048], P('expert'), may hold values from -0.25 to 0.25
- w_second: bfloat16 [8, 2048, 512], P('expert'), may hold values from -1 to 1
- expert_ids: int32 [73728, 2], P(('dp', 'expert')), may hold values from 0 to 7, all different within a row
- priority_ranks: int32 [32, 2304], P(('dp', 'expert')), may hold values from 0 to 2303, each once within a row
- cotangent: float32 [73728, 512], P(('dp', 'expert')), may hold values from -6 to 6
Outputs:
- block_out: bfloat16 [73728, 512], P(('dp', 'expert'))
- grad_tokens: float32 [73728, 512], P(('dp', 'expert'))
- grad_gain_one: float32 [512], replicated
- grad_w_qkv: float32 [512, 1536], replicated
- grad_w_attn_out: float32 [512, 512], replicated
- grad_gain_two: float32 [512], replicated
- grad_w_router: float32 [512, 8], replicated
- grad_w_first: float32 [8, 512, 2048], P('expert')
- grad_w_second: float32 [8, 2048, 512], P('expert')
Inputs may be any that keep to these rules, and one draw needn't show every extreme that they name: `expert_ids`: each row names two different experts, and every expert is named somewhere. `priority_ranks`: each row is a permutation of 0 to 2303.
All inputs are finite; a program needn't handle non-finite values.
Results may differ from a plain program's by a relative error of at most 0.015.
Values may be sent and summed in bfloat16 or wider, within the bound.
No kernel may reach another device: no remote copies, remote signals or barrier semaphores. Data moves between devices by JAX's collectives and lax.ppermute only.
A program may use at most 256 MiB of HBM per device.

v0:
```python
from functools import partial

import jax
import jax.numpy as jnp
from jax import lax
from jax.sharding import PartitionSpec as P

D = 512
HEADS = 8
HEAD_DIM = 64
PATCHES = 144


EPSILON = 1e-06


def layer_norm(values, gain):
    average = jnp.mean(values, axis=-1, keepdims=True)
    centred = values - average
    variance = jnp.mean(centred * centred, axis=-1, keepdims=True)
    return centred * lax.rsqrt(variance + EPSILON) * gain


def route_slots(ids, ranks, experts):
    catalog = jnp.arange(experts, dtype=jnp.int32)
    first_hot = ids[:, 0:1] == catalog
    second_hot = ids[:, 1:2] == catalog
    earlier = (ranks[None, :] < ranks[:, None]).astype(jnp.bfloat16)
    both_hot = jnp.concatenate([first_hot, second_hot], axis=1).astype(jnp.bfloat16)
    counted = jnp.dot(earlier, both_hot, preferred_element_type=jnp.float32)
    first_total = jnp.sum(first_hot.astype(jnp.float32), axis=0)
    slot_first = jnp.sum(jnp.where(first_hot, counted[:, :experts], 0.0), axis=1)
    slot_second = jnp.sum(jnp.where(second_hot, counted[:, experts:] + first_total, 0.0), axis=1)
    return jnp.stack([slot_first, slot_second], axis=1).astype(jnp.int32)


def attention_scores(queries, keys):
    return jnp.einsum(
        "bqhd,bkhd->bhqk", queries, keys, preferred_element_type=jnp.float32
    ) * HEAD_DIM ** (-0.5)


def shards(
    tokens,
    gain_one,
    w_qkv,
    w_attn_out,
    gain_two,
    w_router,
    w_first,
    w_second,
    expert_ids,
    priority_ranks,
    cotangent,
):
    tok_rows = tokens.shape[0]
    experts = w_router.shape[1]
    capacity = max(2, tok_rows // experts)
    images = tok_rows // PATCHES
    scale = HEAD_DIM ** (-0.5)
    highest = lax.Precision.HIGHEST
    inputs = tokens.astype(jnp.float32)
    normed_one, norm_one_back = jax.vjp(layer_norm, inputs, gain_one)
    low_one = normed_one.astype(jnp.bfloat16)
    packed = jnp.dot(low_one, w_qkv, preferred_element_type=jnp.float32).astype(jnp.bfloat16)
    grouped = packed.reshape(images, PATCHES, 3, HEADS, HEAD_DIM)
    queries = grouped[:, :, 0]
    keys = grouped[:, :, 1]
    values = grouped[:, :, 2]
    scores = attention_scores(queries, keys)
    top_score = jnp.max(scores, axis=-1, keepdims=True)
    weights = jnp.exp(scores - top_score)
    totals = jnp.sum(weights, axis=-1, keepdims=True)
    probs = weights / totals
    log_total = top_score + jnp.log(totals)
    mixed = jnp.einsum(
        "bhqk,bkhd->bqhd", probs.astype(jnp.bfloat16), values, preferred_element_type=jnp.float32
    )
    mixed = mixed.reshape(tok_rows, D).astype(jnp.bfloat16)
    resid = inputs + jnp.dot(mixed, w_attn_out, preferred_element_type=jnp.float32)
    normed_two, norm_two_back = jax.vjp(layer_norm, resid, gain_two)
    low_two = normed_two.astype(jnp.bfloat16)
    router_logits = jnp.dot(low_two, w_router, preferred_element_type=jnp.float32)
    router, router_back = jax.vjp(partial(jax.nn.softmax, axis=-1), router_logits)
    slots = route_slots(expert_ids, priority_ranks[0], experts)
    kept = slots < capacity
    keep_float = kept.astype(jnp.float32)
    flat_slot = expert_ids * capacity + slots
    slot_iota = jnp.arange(experts * capacity, dtype=jnp.int32)
    selector = ((flat_slot[:, :, None] == slot_iota) & kept[:, :, None]).astype(jnp.bfloat16)
    dispatch = selector[:, 0] + selector[:, 1]
    outgoing = jnp.einsum(
        "ts,td->sd", dispatch, low_two, preferred_element_type=jnp.float32
    ).astype(jnp.bfloat16)
    received = lax.all_to_all(
        outgoing.reshape(experts, capacity, D), "expert", split_axis=0, concat_axis=1, tiled=True
    )
    pre_act = jnp.einsum("erd,edf->erf", received, w_first, preferred_element_type=jnp.float32)
    activated, gelu_back = jax.vjp(jax.nn.gelu, pre_act)
    hidden = activated.astype(jnp.bfloat16)
    expert_out = jnp.einsum(
        "erf,efd->erd", hidden, w_second, preferred_element_type=jnp.float32
    ).astype(jnp.bfloat16)
    returned = lax.all_to_all(
        expert_out, "expert", split_axis=1, concat_axis=0, tiled=True
    ).reshape(experts * capacity, D)
    gathered = jnp.einsum("tjs,sd->tjd", selector, returned, preferred_element_type=jnp.float32)
    gates = jnp.take_along_axis(router, expert_ids, axis=1) * keep_float
    mixture = jnp.sum(gates[:, :, None] * gathered, axis=1)
    block_out = (resid + mixture).astype(jnp.bfloat16)
    d_gates = jnp.sum(gathered * cotangent[:, None, :], axis=2) * keep_float
    catalog = jnp.arange(experts, dtype=jnp.int32)
    d_router = jnp.sum(
        d_gates[:, :, None] * (expert_ids[:, :, None] == catalog).astype(jnp.float32), axis=1
    )
    d_logits = router_back(d_router)[0]
    router_grad = jnp.einsum("td,te->de", low_two.astype(jnp.float32), d_logits, precision=highest)
    d_norm_router = jnp.einsum(
        "te,de->td", d_logits, w_router.astype(jnp.float32), precision=highest
    )
    scaled = (gates[:, :, None] * cotangent[:, None, :]).astype(jnp.bfloat16)
    d_outgoing = jnp.einsum(
        "tjs,tjd->sd", selector, scaled, preferred_element_type=jnp.float32
    ).astype(jnp.bfloat16)
    d_expert_out = lax.all_to_all(
        d_outgoing.reshape(experts, capacity, D), "expert", split_axis=0, concat_axis=1, tiled=True
    )
    d_hidden = jnp.einsum(
        "erd,efd->erf", d_expert_out, w_second, preferred_element_type=jnp.float32
    )
    d_pre = gelu_back(d_hidden)[0].astype(jnp.bfloat16)
    d_received = jnp.einsum(
        "erf,edf->erd", d_pre, w_first, preferred_element_type=jnp.float32
    ).astype(jnp.bfloat16)
    d_returned = lax.all_to_all(
        d_received, "expert", split_axis=1, concat_axis=0, tiled=True
    ).reshape(experts * capacity, D)
    d_norm_two = d_norm_router + jnp.dot(dispatch, d_returned, preferred_element_type=jnp.float32)
    local_first = jnp.einsum("erd,erf->edf", received, d_pre, preferred_element_type=jnp.float32)
    local_second = jnp.einsum(
        "erf,erd->efd", hidden, d_expert_out, preferred_element_type=jnp.float32
    )
    grad_first, grad_second = (
        lax.psum(local_first.astype(jnp.bfloat16), "dp").astype(jnp.float32),
        lax.psum(local_second.astype(jnp.bfloat16), "dp").astype(jnp.float32),
    )
    d_resid_norm, gain_two_grad = norm_two_back(d_norm_two)
    d_resid = cotangent + d_resid_norm
    d_attn = d_resid.astype(jnp.bfloat16)
    out_grad = jnp.einsum("td,te->de", mixed, d_attn, preferred_element_type=jnp.float32)
    d_mixed = jnp.einsum(
        "te,de->td", d_attn, w_attn_out, preferred_element_type=jnp.float32
    ).astype(jnp.bfloat16)
    d_mixed = d_mixed.reshape(images, PATCHES, HEADS, HEAD_DIM)
    probs_again = jnp.exp(attention_scores(queries, keys) - log_total)
    d_probs = jnp.einsum("bqhd,bkhd->bhqk", d_mixed, values, preferred_element_type=jnp.float32)
    d_values = jnp.einsum(
        "bhqk,bqhd->bkhd",
        probs_again.astype(jnp.bfloat16),
        d_mixed,
        preferred_element_type=jnp.float32,
    )
    inner = jnp.sum(probs_again * d_probs, axis=-1, keepdims=True)
    d_scores = (probs_again * (d_probs - inner)).astype(jnp.bfloat16)
    d_queries = (
        jnp.einsum("bhqk,bkhd->bqhd", d_scores, keys, preferred_element_type=jnp.float32) * scale
    )
    d_keys = (
        jnp.einsum("bhqk,bqhd->bkhd", d_scores, queries, preferred_element_type=jnp.float32) * scale
    )
    d_packed = (
        jnp.stack([d_queries, d_keys, d_values], axis=2)
        .reshape(tok_rows, 3 * D)
        .astype(jnp.bfloat16)
    )
    qkv_grad = jnp.einsum("td,te->de", low_one, d_packed, preferred_element_type=jnp.float32)
    d_norm_one = jnp.einsum("te,de->td", d_packed, w_qkv, preferred_element_type=jnp.float32)
    d_inputs_norm, gain_one_grad = norm_one_back(d_norm_one)
    grad_tokens = d_resid + d_inputs_norm
    summed = lax.psum(
        (qkv_grad, out_grad, router_grad, gain_one_grad, gain_two_grad), ("dp", "expert")
    )
    return (
        block_out,
        grad_tokens,
        summed[3],
        summed[0],
        summed[1],
        summed[4],
        summed[2],
        grad_first,
        grad_second,
    )


def solution(mesh):
    in_specs = (
        P(("dp", "expert"), None),
        P(),
        P(),
        P(),
        P(),
        P(),
        P("expert", None, None),
        P("expert", None, None),
        P(("dp", "expert"), None),
        P(("dp", "expert"), None),
        P(("dp", "expert"), None),
    )
    out_specs = (
        P(("dp", "expert"), None),
        P(("dp", "expert"), None),
        P(),
        P(),
        P(),
        P(),
        P(),
        P("expert", None, None),
        P("expert", None, None),
    )
    return jax.shard_map(shards, mesh=mesh, in_specs=in_specs, out_specs=out_specs, check_vma=False)
```

profile of v0, /device:TPU:0, one launch (start us, length us, event | category | flops | bytes accessed | tf_op | source)
XLA Modules:
  0.0 840.1 jit_solution(9506455554479038517)
XLA Ops:
  40.4 18.0 %reshape.274 = bf16[16,144,3,8,64]{4,3,2,1,0:T(8,128)(2,1)} reshape(bf16[2304,1536]{1,0:T(8,128)(2,1)} %convolution_convert_fusion) | data formatting | bytes 14155776 | tf_op jit(solution)/shard_map/reshape | solution.py:66
  58.4 13.0 %fusion.104 = (bf16[16,144,1,8,64]{4,3,2,1,0:T(8,128)(2,1)}, bf16[16,144,1,8,64]{4,3,2,1,0:T(8,128)(2,1)}, bf16[16,144,1,8,64]{4,3,2,1,0:T(8,128)(2,1)}) fusion(bf16[16,144,3,8,64]{4,3,2,1,0:T(8,128)(2,1)} %reshape.274), kind=kLoop, calls=%fused_computation.154 | loop fusion | bytes 14155776 | tf_op jit(solution)/shard_map/slice | solution.py:69
  94.9 12.7 %multiply_reduce_fusion.1 = (f32[16,8,144]{2,1,0:T(8,128)S(1)}, f32[16,8,144,144]{2,3,1,0:T(8,128)}) fusion(bf16[16,144,1,8,64]{1,4,3,0,2:T(8,128)(2,1)} %copy.188, bf16[16,144,1,8,64]{1,4,3,0,2:T(8,128)(2,1)} %copy.187), kind=kOutput, calls=%fused_computation.28 | convolution fusion | flops 345028608 | bytes 15409152 | tf_op jit(solution)/shard_map/bqhd,bkhd->bhqk/dot_general | solution.py:38
  107.6 11.8 %fusion.19 = f32[16,8,144]{2,1,0:T(8,128)S(1)} fusion(f32[16,8,144,144]{2,3,1,0:T(8,128)} %get-tuple-element.91, f32[16,8,144]{2,1,0:T(8,128)S(1)} %get-tuple-element.90), kind=kLoop, calls=%fused_computation.27 | loop fusion | flops 7944192 | bytes 10764288 | tf_op jit(solution)/shard_map/reduce_sum | solution.py:73
  119.5 10.6 %convert_bitcast_fusion.1 = bf16[16,144,8,64]{1,3,2,0:T(8,128)(2,1)S(1)} fusion(f32[16,8,144,144]{2,3,1,0:T(8,128)} %get-tuple-element.91, f32[16,8,144]{2,1,0:T(8,128)S(1)} %fusion.19, f32[16,8,144]{2,1,0:T(8,128)S(1)} %get-tuple-element.90, bf16[16,144,1,8,64]{1,4,3,0,2:T(8,128)(2,1)} %copy.186), kind=kOutput, calls=%fused_computation.89 | convolution fusion | flops 351535104 | bytes 15482880 | tf_op jit(solution)/shard_map/bhqk,bkhd->bqhd/dot_general | solution.py:76
  151.0 27.0 %gather_fusion = f32[4608]{0:T(1024)S(1)} fusion(f32[2304,8]{0,1:T(8,128)S(1)} %fusion.94, s32[4608]{0:T(1024)S(1)} %reshape.261), kind=kCustom, calls=%fused_computation | custom fusion | bytes 73728 | tf_op jit(solution)/shard_map/jit(take_along_axis)/gather | solution.py:108
  179.7 15.2 %fusion.44 = bf16[2304,512]{1,0:T(8,128)(2,1)} fusion(f32[2304,512]{0,1:T(8,128)} %copy.165, f32[2304,2]{0,1:T(2,128)S(1)} %get-tuple-element.82, s32[2304,2]{0,1:T(2,128)S(1)} %multiply_add_fusion, pred[2304,2]{0,1:T(4,128)(4,1)S(1)} %get-tuple-element.83), kind=kOutput, calls=%fused_computation.71 | convolution fusion | flops 10898767872 | bytes 7119360 | tf_op jit(solution)/shard_map/tjs,tjd->sd/dot_general | solution.py:122
  201.3 10.1 %fusion.5 = bf16[2304,2,2304]{0,2,1:T(8,128)(2,1)} fusion(s32[2304,2]{0,1:T(2,128)S(1)} %multiply_add_fusion, pred[2304,2]{0,1:T(4,128)(4,1)S(1)} %get-tuple-element.83), kind=kLoop, calls=%fused_computation.5 | loop fusion | flops 31850496 | bytes 21256704 | tf_op jit(solution)/shard_map/convert_element_type | solution.py:90
  211.3 11.1 %convolution_convert_fusion.4 = bf16[2304,512]{1,0:T(8,128)(2,1)} fusion(bf16[2304,512]{0,1:T(8,128)(2,1)S(1)} %copy-done.7, bf16[2304,2,2304]{0,2,1:T(8,128)(2,1)} %fusion.5), kind=kOutput, calls=%fused_computation.75 | convolution fusion | flops 5442306048 | bytes 25952256 | tf_op jit(solution)/shard_map/ts,td->sd/dot_general | solution.py:92
  222.4 33.6 %all-to-all-done.2 = bf16[8,288,512]{2,1,0:T(8,128)(2,1)} async-done(((bf16[8,288,512]{2,1,0:T(8,128)(2,1)}), bf16[8,288,512]{2,1,0:T(8,128)(2,1)}, u32[]{:S(2)}, u32[]{:S(2)}) %all-to-all-start.2) | async-done | bytes 2359328 | tf_op jit(solution)/shard_map/all_to_all | solution.py:125
  260.6 11.0 %fusion.75 = f32[2304,2048]{1,0:T(8,128)} fusion(bf16[2304,512]{1,0:T(8,128)(2,1)} %bitcast.15, bf16[1,2048,512]{2,1,0:T(8,128)(2,1)} %param.18), kind=kOutput, calls=%fused_computation.100 | convolution fusion | flops 4831838208 | bytes 23330816 | tf_op jit(solution)/shard_map/erd,efd->erf/dot_general | solution.py:128
  271.6 43.7 %all-to-all-done = bf16[8,288,512]{2,1,0:T(8,128)(2,1)} async-done(((bf16[8,288,512]{2,1,0:T(8,128)(2,1)}), bf16[8,288,512]{2,1,0:T(8,128)(2,1)}, u32[]{:S(2)}, u32[]{:S(2)}) %all-to-all-start) | async-done | bytes 2359328 | tf_op jit(solution)/shard_map/all_to_all | solution.py:95
  315.3 22.0 %fusion.18 = (bf16[2304,2048]{1,0:T(8,128)(2,1)S(1)}, bf16[2304,2048]{1,0:T(8,128)(2,1)}) fusion(f32[2304,2048]{1,0:T(8,128)} %fusion.75, bf16[2304,512]{1,0:T(8,128)(2,1)} %bitcast.7, bf16[1,512,2048]{2,1,0:T(8,128)(2,1)S(1)} %copy-done), kind=kOutput, calls=%fused_computation.20 | convolution fusion | flops 4935647232 | bytes 42205184 | tf_op jit(solution)/shard_map/erd,edf->erf/dot_general | solution.py:98
  342.9 20.8 %copy.195 = bf16[1,2304,512]{2,0,1:T(2,128)(2,1)} copy(bf16[1,2304,512]{2,1,0:T(8,128)(2,1)S(1)} %fusion.60) | data formatting | bytes 4718592 | tf_op jit(solution)/shard_map/convert_element_type | solution.py:134
  364.2 17.4 %reduce.5 = bf16[2304,512]{1,0:T(8,128)(2,1)} reduce(bf16[2304,1,512]{2,1,0:T(2,128)(2,1)} %bitcast.133, bf16[]{:T(256)} %broadcast.238), dimensions={1}, to_apply=%bitcast.127.reduce_sub_computation | reduce | bytes 4718594
  392.7 9.3 %fusion.59 = bf16[1,2304,512]{2,1,0:T(8,128)(2,1)S(1)} fusion(bf16[2304,2048]{1,0:T(8,128)(2,1)} %get-tuple-element.85, bf16[1,2048,512]{2,1,0:T(8,128)(2,1)} %param.18), kind=kOutput, calls=%fused_computation.90 | convolution fusion | flops 4833017856 | bytes 13893632 | tf_op jit(solution)/shard_map/erf,efd->erd/dot_general | solution.py:101
  402.0 20.8 %copy.196 = bf16[1,2304,512]{2,0,1:T(2,128)(2,1)} copy(bf16[1,2304,512]{2,1,0:T(8,128)(2,1)S(1)} %fusion.59) | data formatting | bytes 4718592 | tf_op jit(solution)/shard_map/convert_element_type | solution.py:103
  422.8 17.0 %reduce.6 = bf16[2304,512]{1,0:T(8,128)(2,1)} reduce(bf16[2304,1,512]{2,1,0:T(2,128)(2,1)} %bitcast.134, bf16[]{:T(256)} %broadcast.238), dimensions={1}, to_apply=%bitcast.128.reduce_sub_computation | reduce | bytes 4718594
  451.7 9.4 %fusion.61 = bf16[1,512,2048]{2,1,0:T(8,128)(2,1)} fusion(bf16[2304,512]{1,0:T(8,128)(2,1)} %bitcast.7, bf16[2304,2048]{1,0:T(8,128)(2,1)} %copy-done.48), kind=kOutput, calls=%fused_computation.94 | convolution fusion | flops 4832886784 | bytes 13893632 | tf_op jit(solution)/shard_map/erd,erf->edf/dot_general | solution.py:139
  461.1 9.4 %fusion.62 = bf16[1,2048,512]{2,1,0:T(8,128)(2,1)} fusion(bf16[2304,2048]{1,0:T(8,128)(2,1)} %get-tuple-element.85, bf16[2304,512]{1,0:T(8,128)(2,1)} %bitcast.15), kind=kOutput, calls=%fused_computation.95 | convolution fusion | flops 4832886784 | bytes 13893632 | tf_op jit(solution)/shard_map/erf,erd->efd/dot_general | solution.py:140
  477.7 13.9 %fusion.71 = f32[2304,512]{0,1:T(8,128)} fusion(bf16[1,2304,512]{2,0,1:T(2,128)(2,1)} %bitcast.136, bf16[2304,2,2304]{0,2,1:T(8,128)(2,1)} %fusion.5), kind=kOutput, calls=%fused_computation.96 | convolution fusion | flops 5441126400 | bytes 28311552 | tf_op jit(solution)/shard_map/dot_general | solution.py:138
  491.6 14.7 %all-to-all-done.1 = bf16[8,2,73728]{2,1,0:T(2,128)(2,1)} async-done(((bf16[8,2,73728]{2,1,0:T(2,128)(2,1)}), bf16[8,2,73728]{2,1,0:T(2,128)(2,1)}, u32[]{:S(2)}, u32[]{:S(2)}) %all-to-all-start.1) | async-done | bytes 2359328 | tf_op jit(solution)/shard_map/all_to_all | solution.py:104
  513.5 11.0 %copy.160 = bf16[1,2304,512]{1,2,0:T(8,128)(2,1)} copy(bf16[1,2304,512]{2,0,1:T(2,128)(2,1)} %bitcast.135) | data formatting | bytes 4718592 | tf_op jit(solution)/shard_map/all_to_all | solution.py:104
  524.6 19.4 %multiply_reduce_fusion.2 = (f32[2304,2]{0,1:T(2,128)S(1)}, f32[2304,512]{0,1:T(8,128)}) fusion(f32[2304,512]{0,1:T(8,128)} %copy.165, f32[2304,2]{0,1:T(2,128)S(1)} %get-tuple-element.82, bf16[1,2304,512]{1,2,0:T(8,128)(2,1)} %copy.160, s32[2304,2]{0,1:T(2,128)S(1)} %multiply_add_fusion, pred[2304,2]{0,1:T(4,128)(4,1)S(1)} %get-tuple-element.83), kind=kOutput, calls=%fused_computation.39 | convolution fusion | flops 10901123072 | bytes 11856384 | tf_op jit(solution)/shard_map/tjs,sd->tjd/dot_general | solution.py:107
  574.2 11.6 %convert_bitcast_fusion = bf16[16,144,1,8,64]{1,4,3,0,2:T(8,128)(2,1)} fusion(bf16[16,144,8,64]{1,3,2,0:T(8,128)(2,1)} %copy.167, f32[16,8,144,144]{2,3,1,0:T(8,128)} %get-tuple-element.91, f32[16,8,144]{2,1,0:T(8,128)S(1)} %log_add_fusion), kind=kOutput, calls=%fused_computation.88 | convolution fusion | flops 348880896 | bytes 15409152 | tf_op jit(solution)/shard_map/bhqk,bqhd->bkhd/dot_general | solution.py:157
  585.8 16.1 %multiply_reduce_fusion = (f32[16,8,144]{2,1,0:T(8,128)S(1)}, f32[16,8,144,144]{2,3,1,0:T(8,128)}) fusion(f32[16,8,144,144]{2,3,1,0:T(8,128)} %get-tuple-element.91, f32[16,8,144]{2,1,0:T(8,128)S(1)} %log_add_fusion, bf16[16,144,8,64]{1,3,2,0:T(8,128)(2,1)} %copy.167, bf16[16,144,1,8,64]{1,4,3,0,2:T(8,128)(2,1)} %copy.186), kind=kOutput, calls=%fused_computation.22 | convolution fusion | flops 350337024 | bytes 26099712 | tf_op jit(solution)/shard_map/bqhd,bkhd->bhqk/dot_general | solution.py:156
  601.8 13.7 %multiply_convert_fusion = bf16[16,8,144,144]{2,3,1,0:T(8,128)(2,1)S(1)} fusion(f32[16,8,144,144]{2,3,1,0:T(8,128)} %get-tuple-element.98, f32[16,8,144,144]{2,3,1,0:T(8,128)} %get-tuple-element.91, f32[16,8,144]{2,1,0:T(8,128)S(1)} %get-tuple-element.97, f32[16,8,144]{2,1,0:T(8,128)S(1)} %log_add_fusion), kind=kLoop, calls=%fused_computation.21 | loop fusion | flops 13271040 | bytes 26689536 | tf_op jit(solution)/shard_map/convert_element_type | solution.py:164
  622.6 10.1 %fusion.48 = bf16[16,144,1,8,64]{1,4,3,0,2:T(8,128)(2,1)} fusion(bf16[16,8,144,144]{2,3,1,0:T(8,128)(2,1)} %copy-done.2, bf16[16,144,1,8,64]{1,4,3,0,2:T(8,128)(2,1)} %copy.187), kind=kOutput, calls=%fused_computation.77 | convolution fusion | flops 342097920 | bytes 10027008 | tf_op jit(solution)/shard_map/bhqk,bqhd->bkhd/dot_general | solution.py:169
  647.6 21.1 %convert_element_type.138 = bf16[2304,1536]{0,1:T(8,128)(2,1)} reshape(bf16[16,144,3,8,64]{1,0,4,3,2:T(8,128)(2,1)} %copy.172) | data formatting | bytes 14155776 | tf_op jit(solution)/shard_map/convert_element_type | solution.py:174
  668.8 10.3 %fusion.41 = (f32[2304]{0:T(1024)S(1)}, f32[2304,512]{0,1:T(8,128)}) fusion(bf16[2304,512]{0,1:T(8,128)(2,1)} %copy.150, f32[512]{0:T(512)S(1)} %copy-done.47, f32[2304]{0:T(1024)S(1)} %copy-done.31, bf16[512,1536]{1,0:T(8,128)(2,1)} %param.13, bf16[2304,1536]{0,1:T(8,128)(2,1)} %convert_element_type.138), kind=kOutput, calls=%fused_computation.61 | convolution fusion | flops 3629774592 | bytes 15749120 | tf_op jit(solution)/shard_map/te,de->td/dot_general | solution.py:177
  715.9 38.7 %all-reduce = (f32[512]{0:T(512)}, f32[512]{0:T(512)}, f32[512,8]{0,1:T(8,128)}) all-reduce(f32[512]{0:T(512)S(1)} %get-tuple-element.67, f32[512]{0:T(512)S(1)} %get-tuple-element.63, f32[512,8]{0,1:T(8,128)S(1)} %fusion.102), channel_id=1, replica_groups=mesh['dp'=4,'expert'=8] {'dp','expert'}, use_global_device_ids=true, to_apply=%region_21.22 | all-reduce | flops 5120 | bytes 40960 | tf_op jit(solution)/shard_map/psum | solution.py:180
  761.5 66.8 %all-reduce.6.cloned.1.call-done = (f32[512,1536]{1,0:T(8,128)}, f32[512,512]{1,0:T(8,128)}) async-done(((f32[512,1536]{1,0:T(8,128)}, f32[512,512]{1,0:T(8,128)}), (f32[512,1536]{1,0:T(8,128)}, f32[512,512]{1,0:T(8,128)})) %all-reduce.6.cloned.1.call-update) | async-done | bytes 4194320 | tf_op jit(solution)/shard_map/psum | solution.py:180
  (194 shorter events, 233.8 us)
Async XLA Ops:
  7.2 308.1 %copy-start = (bf16[1,512,2048]{2,1,0:T(8,128)(2,1)S(1)}, bf16[1,512,2048]{2,1,0:T(8,128)(2,1)}, u32[]{:S(2)}) copy-start(bf16[1,512,2048]{2,1,0:T(8,128)(2,1)} %param.17) | copy-start | bytes 6291460
  107.6 11.8 %copy-start.15 = (f32[16,8,144]{2,1,0:T(8,128)}, f32[16,8,144]{2,1,0:T(8,128)S(1)}, u32[]{:S(2)}) copy-start(f32[16,8,144]{2,1,0:T(8,128)S(1)} %get-tuple-element.90) | copy-start | bytes 221188
  119.5 10.7 %copy-start.18 = (f32[16,8,144]{2,1,0:T(8,128)}, f32[16,8,144]{2,1,0:T(8,128)S(1)}, u32[]{:S(2)}) copy-start(f32[16,8,144]{2,1,0:T(8,128)S(1)} %fusion.19) | copy-start | bytes 221188
  151.0 28.6 %copy-start.22 = (s32[2304,2]{0,1:T(2,128)S(1)}, s32[2304,2]{0,1:T(2,128)}, u32[]{:S(2)}) copy-start(s32[2304,2]{0,1:T(2,128)} %param.19) | copy-start | bytes 55300
  151.0 28.6 %copy-start.40 = (f32[2304,1]{0,1:T(1,128)S(1)}, f32[2304,1]{0,1:T(1,128)}, u32[]{:S(2)}) copy-start(f32[2304,1]{0,1:T(1,128)} %stack.25) | copy-start | bytes 27652
  151.0 28.6 %copy-start.41 = (f32[2304,1]{0,1:T(1,128)S(1)}, f32[2304,1]{0,1:T(1,128)}, u32[]{:S(2)}) copy-start(f32[2304,1]{0,1:T(1,128)} %stack.26) | copy-start | bytes 27652
  194.9 61.1 %all-to-all-start.2 = ((bf16[8,288,512]{2,1,0:T(8,128)(2,1)}), bf16[8,288,512]{2,1,0:T(8,128)(2,1)}, u32[]{:S(2)}, u32[]{:S(2)}) async-start(bf16[8,288,512]{2,1,0:T(8,128)(2,1)} %bitcast.140), calls=%async_computation.2 | async-start | bytes 4718592 | tf_op jit(solution)/shard_map/all_to_all | solution.py:125
  201.3 10.1 %copy-start.7 = (bf16[2304,512]{0,1:T(8,128)(2,1)S(1)}, bf16[2304,512]{0,1:T(8,128)(2,1)}, u32[]{:S(2)}) copy-start(bf16[2304,512]{0,1:T(8,128)(2,1)} %copy-done.6) | copy-start | bytes 7077892
  256.1 59.3 %all-to-all-start = ((bf16[8,288,512]{2,1,0:T(8,128)(2,1)}), bf16[8,288,512]{2,1,0:T(8,128)(2,1)}, u32[]{:S(2)}, u32[]{:S(2)}) async-start(bf16[8,288,512]{2,1,0:T(8,128)(2,1)} %bitcast.139), calls=%async_computation | async-start | bytes 4718592 | tf_op jit(solution)/shard_map/all_to_all | solution.py:95
  381.6 11.0 %copy-start.29 = (f32[2304]{0:T(1024)S(1)}, f32[2304]{0:T(1024)}, u32[]{:S(2)}) copy-start(f32[2304]{0:T(1024)} %copy-done.28) | copy-start | bytes 27652
  381.6 11.0 %copy-start.16 = (f32[16,8,144]{2,1,0:T(8,128)S(1)}, f32[16,8,144]{2,1,0:T(8,128)}, u32[]{:S(2)}) copy-start(f32[16,8,144]{2,1,0:T(8,128)} %copy-done.15) | copy-start | bytes 221188
  381.6 11.0 %copy-start.19 = (f32[16,8,144]{2,1,0:T(8,128)S(1)}, f32[16,8,144]{2,1,0:T(8,128)}, u32[]{:S(2)}) copy-start(f32[16,8,144]{2,1,0:T(8,128)} %copy-done.18) | copy-start | bytes 221188
  388.2 59.1 %all-to-all-start.3 = ((bf16[8,2,73728]{2,1,0:T(2,128)(2,1)}), bf16[8,2,73728]{2,1,0:T(2,128)(2,1)}, u32[]{:S(2)}, u32[]{:S(2)}) async-start(bf16[8,2,73728]{2,1,0:T(2,128)(2,1)} %reshape.281), calls=%async_computation.3 | async-start | bytes 4718592 | tf_op jit(solution)/shard_map/all_to_all | solution.py:135
  447.3 59.1 %all-to-all-start.1 = ((bf16[8,2,73728]{2,1,0:T(2,128)(2,1)}), bf16[8,2,73728]{2,1,0:T(2,128)(2,1)}, u32[]{:S(2)}, u32[]{:S(2)}) async-start(bf16[8,2,73728]{2,1,0:T(2,128)(2,1)} %reshape.279), calls=%async_computation.1 | async-start | bytes 4718592 | tf_op jit(solution)/shard_map/all_to_all | solution.py:104
  451.7 303.0 %all-reduce.8.cloned.1.call-start = ((), (), s32[]{:S(2)}) async-start(), calls=%async_computation.5 | async-start | bytes 8388608 | tf_op jit(solution)/shard_map/psum | solution.py:144
  470.5 357.8 %all-reduce.6.cloned.1.call-start = ((), (), s32[]{:S(2)}) async-start(), calls=%async_computation.4 | async-start | bytes 8388608 | tf_op jit(solution)/shard_map/psum | solution.py:180
  513.5 30.6 %slice-start = ((s8[4718592]{0:T(1024)(128)(4,1)}), s8[524288]{0:T(1024)(128)(4,1)S(1)}, s32[]{:S(2)}) async-start(s8[4718592]{0:T(1024)(128)(4,1)} %bitcast.129), calls=%async_computation.6 | async-start | bytes 1048576
  524.5 19.4 %copy-start.23 = (s32[2304,2]{0,1:T(2,128)S(1)}, s32[2304,2]{0,1:T(2,128)}, u32[]{:S(2)}) copy-start(s32[2304,2]{0,1:T(2,128)} %param.19) | copy-start | bytes 55300
  524.5 19.5 %copy-start.11 = (f32[2304,8]{0,1:T(8,128)S(1)}, f32[2304,8]{0,1:T(8,128)}, u32[]{:S(2)}) copy-start(f32[2304,8]{0,1:T(8,128)} %copy-done.10) | copy-start | bytes 221188
  524.5 19.5 %copy-start.25 = (f32[2304]{0:T(1024)S(1)}, f32[2304]{0:T(1024)}, u32[]{:S(2)}) copy-start(f32[2304]{0:T(1024)} %copy-done.24) | copy-start | bytes 27652
  524.5 19.6 %slice-start.1 = ((s8[4718592]{0:T(1024)(128)(4,1)}), s8[4194304]{0:T(1024)(128)(4,1)S(1)}, s32[]{:S(2)}) async-start(s8[4718592]{0:T(1024)(128)(4,1)} %bitcast.129), calls=%async_computation.7 | async-start | bytes 8388608
  524.5 19.6 %copy-start.27 = (f32[2304]{0:T(1024)S(1)}, f32[2304]{0:T(1024)}, u32[]{:S(2)}) copy-start(f32[2304]{0:T(1024)} %copy-done.26) | copy-start | bytes 27652
  524.5 19.6 %copy-start.33 = (f32[2304]{0:T(1024)S(1)}, f32[2304]{0:T(1024)}, u32[]{:S(2)}) copy-start(f32[2304]{0:T(1024)} %copy-done.32) | copy-start | bytes 27652
  524.5 19.6 %copy-start.43 = (bf16[512,8]{0,1:T(8,128)(2,1)S(1)}, bf16[512,8]{0,1:T(8,128)(2,1)}, u32[]{:S(2)}) copy-start(bf16[512,8]{0,1:T(8,128)(2,1)} %param.16) | copy-start | bytes 24580
  524.6 19.6 %copy-start.45 = (f32[512]{0:T(512)S(1)}, f32[512]{0:T(512)}, u32[]{:S(2)}) copy-start(f32[512]{0:T(512)} %param.15) | copy-start | bytes 6148
  601.8 17.3 %copy-start.4 = (bf16[16,144,1,8,64]{1,4,3,0,2:T(8,128)(2,1)S(1)}, bf16[16,144,1,8,64]{1,4,3,0,2:T(8,128)(2,1)}, u32[]{:S(2)}) copy-start(bf16[16,144,1,8,64]{1,4,3,0,2:T(8,128)(2,1)} %copy.188) | copy-start | bytes 7077892
  647.6 21.1 %copy-start.31 = (f32[2304]{0:T(1024)S(1)}, f32[2304]{0:T(1024)}, u32[]{:S(2)}) copy-start(f32[2304]{0:T(1024)} %copy-done.30) | copy-start | bytes 27652
  647.6 21.1 %copy-start.47 = (f32[512]{0:T(512)S(1)}, f32[512]{0:T(512)}, u32[]{:S(2)}) copy-start(f32[512]{0:T(512)} %param.12) | copy-start | bytes 6148
  668.7 10.4 %copy-start.37 = (f32[2304]{0:T(1024)S(1)}, f32[2304]{0:T(1024)}, u32[]{:S(2)}) copy-start(f32[2304]{0:T(1024)} %copy-done.36) | copy-start | bytes 27652
  668.7 10.4 %copy-start.8 = (bf16[2304,512]{0,1:T(8,128)(2,1)S(1)}, bf16[2304,512]{0,1:T(8,128)(2,1)}, u32[]{:S(2)}) copy-start(bf16[2304,512]{0,1:T(8,128)(2,1)} %convert_element_type.119) | copy-start | bytes 7077892
  668.7 10.4 %copy-start.13 = (bf16[2304,512]{0,1:T(8,128)(2,1)S(1)}, bf16[2304,512]{0,1:T(8,128)(2,1)}, u32[]{:S(2)}) copy-start(bf16[2304,512]{0,1:T(8,128)(2,1)} %copy-done.12) | copy-start | bytes 7077892
  668.7 12.7 %copy-start.9 = (bf16[2304,1536]{0,1:T(8,128)(2,1)S(1)}, bf16[2304,1536]{0,1:T(8,128)(2,1)}, u32[]{:S(2)}) copy-start(bf16[2304,1536]{0,1:T(8,128)(2,1)} %convert_element_type.138) | copy-start | bytes 21233668
  (29 other events, 101.2 us)
Sparse Core Ops, SparseCore 0:
  470.6 105.4 all-reduce.7
  687.2 141.0 all-reduce.5
where the time goes:
time: 848 us; the launch traced here: 840 us
  local copies, waits for them, and re-layouts  260 us (31%)
  matrix products  238 us (28%)
  waiting for transfers between devices  160 us (19%)
  other arithmetic  109 us (13%)
  blocking collectives  38.7 us (5%)
  starting transfers between devices  19.7 us (2%)
  between operations  15 us (2%)
    unnamed x124, local copies, waits for them, and re-layouts  87.4 us
    psum x1, waiting for transfers between devices, shards(): lax.psum((qkv_grad, out_grad, router_grad, gain_one_grad, gain_two_grad),...  66.8 us
    all_to_all x1, waiting for transfers between devices, shards(): lax.all_to_all(outgoing.reshape(experts, capacity, D), 'expert', split_ax...  43.7 us
    psum x1, blocking collectives, shards(): lax.psum((qkv_grad, out_grad, router_grad, gain_one_grad, gain_two_grad),...  38.7 us
    unnamed x6, other arithmetic  35.2 us
    all_to_all x1, waiting for transfers between devices, shards(): lax.all_to_all(d_outgoing.reshape(experts, capacity, D), 'expert', split_...  33.6 us
    gather x5, local copies, waits for them, and re-layouts, shards(): gates = jnp.take_along_axis(router, expert_ids, axis=1) * keep_float  29.5 us
    dot_general x1, matrix products, shards(): jnp.einsum('erd,edf->erf', received, w_first, preferred_element_type=jnp....  22 us
  transfers between devices with their start and end apart: 6, of which 5 were waited for; matrix products, arithmetic and copies ran while one was open for 40% of the time, Pallas kernels for 0%

commit v1 on v0

v1 whole, which is shorter than its diff:
```python
from functools import partial

import jax
import jax.numpy as jnp
from jax import lax
from jax.experimental import pallas as pl
from jax.experimental.pallas import tpu as pltpu
from jax.sharding import PartitionSpec as P

D = 512
HEADS = 8
HEAD_DIM = 64
PATCHES = 144
QUAD = 256
EPSILON = 1e-06
EXTRA = 16
LANES = 128
F32 = jnp.float32
BF16 = jnp.bfloat16
VMEM_LIMIT = 60 * 1024 * 1024


def nn(a, b):
    return lax.dot_general(a, b, (((1,), (0,)), ((), ())), preferred_element_type=F32)


def nt(a, b):
    return lax.dot_general(a, b, (((1,), (1,)), ((), ())), preferred_element_type=F32)


def tn(a, b):
    return lax.dot_general(a, b, (((0,), (0,)), ((), ())), preferred_element_type=F32)


def standardise(values):
    average = jnp.mean(values, axis=-1, keepdims=True)
    centred = values - average
    variance = jnp.mean(centred * centred, axis=-1, keepdims=True)
    inverse = lax.rsqrt(variance + EPSILON)
    return centred * inverse, inverse


def standardise_back(hat, inverse, gain, grad):
    scaled = grad * gain
    mean_one = jnp.mean(scaled, axis=-1, keepdims=True)
    mean_two = jnp.mean(scaled * hat, axis=-1, keepdims=True)
    return inverse * (scaled - mean_one - hat * mean_two)


def halves(values):
    high = values.astype(BF16)
    low = (values - high.astype(F32)).astype(BF16)
    return high, low


def params(**more):
    return pltpu.CompilerParams(vmem_limit_bytes=VMEM_LIMIT, **more)


def whole(shape):
    zeros = (0,) * len(shape)
    return pl.BlockSpec(shape, lambda *_: zeros)


def route_kernel(experts, capacity, stride, ids_ref, ranks_ref, out_ref, cols_ref):
    toks = ids_ref.shape[1]
    catalog = lax.broadcasted_iota(jnp.int32, (experts, toks), 0)
    first_hot = (ids_ref[0:1, :] == catalog).astype(F32)
    second_hot = (ids_ref[1:2, :] == catalog).astype(F32)
    both = jnp.concatenate([first_hot, second_hot], axis=0).astype(BF16)
    first_total = jnp.sum(first_hot, axis=1, keepdims=True)
    ranks = ranks_ref[...].astype(F32)
    rank_rows = jnp.broadcast_to(ranks, (8, toks))
    rank_cols = jnp.transpose(rank_rows)[:, 0:1]
    tile = 256
    for start in range(0, toks, tile):
        part = slice(start, start + tile)
        earlier = (rank_cols < ranks[:, part]).astype(F32).astype(BF16)
        counted = nn(both, earlier)
        slot_first = jnp.sum(counted[:experts] * first_hot[:, part], axis=0, keepdims=True)
        slot_second = jnp.sum(
            (counted[experts:] + first_total) * second_hot[:, part], axis=0, keepdims=True
        )
        for row, slot in ((0, slot_first), (1, slot_second)):
            slot = slot.astype(jnp.int32)
            flat = ids_ref[row : row + 1, part] * stride + slot
            out_ref[row : row + 1, part] = jnp.where(slot < capacity, flat, -1)
    out_ref[2:, :] = jnp.full((6, toks), -1, jnp.int32)
    cols_ref[...] = jnp.transpose(out_ref[...].astype(F32)).astype(jnp.int32)


def route(ids, ranks, experts, capacity, stride):
    toks = ranks.shape[1]
    return pl.pallas_call(
        partial(route_kernel, experts, capacity, stride),
        out_shape=(
            jax.ShapeDtypeStruct((8, toks), jnp.int32),
            jax.ShapeDtypeStruct((toks, 8), jnp.int32),
        ),
        in_specs=[whole((2, toks)), whole((1, toks))],
        out_specs=(whole((8, toks)), whole((toks, 8))),
        grid=(1,),
        compiler_params=params(),
        name="route",
        cost_estimate=pl.CostEstimate(
            flops=2 * toks * toks * 128, bytes_accessed=toks * 48, transcendentals=0
        ),
    )(ids, ranks)


def selector_rows(base, rows, flat_ref):
    toks = flat_ref.shape[1]
    slot = lax.broadcasted_iota(jnp.int32, (rows, toks), 0) + base
    hit = (slot == flat_ref[0:1, :]) | (slot == flat_ref[1:2, :])
    return jnp.where(hit, 1.0, 0.0).astype(BF16)


def dispatch_grad_kernel(stride, flat_ref, grad_ref, out_ref, low_ref):
    expert = pl.program_id(0)

    @pl.when(expert == 0)
    def _():
        low_ref[...] = grad_ref[...].astype(BF16)

    chosen = selector_rows(expert * stride, out_ref.shape[1], flat_ref)
    out_ref[0] = nn(chosen, low_ref[...]).astype(BF16)


def dispatch_grad(flat, grad, experts, rows, stride):
    toks = grad.shape[0]
    return pl.pallas_call(
        partial(dispatch_grad_kernel, stride),
        out_shape=jax.ShapeDtypeStruct((experts, rows, D), BF16),
        in_specs=[whole((8, toks)), whole((toks, D))],
        out_specs=pl.BlockSpec((1, rows, D), lambda e: (e, 0, 0)),
        grid=(experts,),
        scratch_shapes=[pltpu.VMEM((toks, D), BF16)],
        compiler_params=params(),
        name="dispatch_grad",
        cost_estimate=pl.CostEstimate(
            flops=2 * toks * experts * rows * D, bytes_accessed=toks * D * 6, transcendentals=0
        ),
    )(flat, grad)


def dispatch_kernel(stride, rows, flat_ref, low_ref, router_ref, out_ref, split_ref):
    expert = pl.program_id(0)
    experts = pl.num_programs(0)

    @pl.when(expert == 0)
    def _():
        router = router_ref[...]
        high, low = halves(router)
        split_ref[:, :LANES] = high
        split_ref[:, LANES:] = low

    chosen = selector_rows(expert * stride, rows, flat_ref)
    out_ref[0, :rows] = nn(chosen, low_ref[...]).astype(BF16)
    picked = nn(chosen, split_ref[...])
    lane = lax.broadcasted_iota(jnp.int32, (rows, LANES), 1)
    here = lane == expert
    high = jnp.sum(jnp.where(here, picked[:, :LANES], 0.0), axis=1, keepdims=True)
    low = jnp.sum(jnp.where(here, picked[:, LANES:], 0.0), axis=1, keepdims=True)
    wide = jnp.where(lane == 0, high, jnp.where(lane == 1, low, 0.0))
    out_ref[0, rows:] = rows_of(wide, rows)


def rows_of(wide, rows):
    flipped = jnp.transpose(wide)[:EXTRA]
    return jnp.concatenate([flipped, jnp.zeros((EXTRA, D - rows), F32)], axis=1).astype(BF16)


def columns_of(extra, rows):
    flipped = jnp.transpose(extra.astype(F32))
    return flipped[:rows, 0:1] + flipped[:rows, 1:2]


def dispatch(flat, low, router, experts, rows, stride):
    toks = low.shape[0]
    return pl.pallas_call(
        partial(dispatch_kernel, stride, rows),
        out_shape=jax.ShapeDtypeStruct((experts, stride, D), BF16),
        in_specs=[whole((8, toks)), whole((toks, D)), whole((toks, LANES))],
        out_specs=pl.BlockSpec((1, stride, D), lambda e: (e, 0, 0)),
        grid=(experts,),
        scratch_shapes=[pltpu.VMEM((toks, 2 * LANES), BF16)],
        compiler_params=params(),
        name="dispatch",
        cost_estimate=pl.CostEstimate(
            flops=2 * toks * experts * rows * (D + 256),
            bytes_accessed=toks * D * 6,
            transcendentals=0,
        ),
    )(flat, low, router)


def head_stack(values):
    lane = lax.broadcasted_iota(jnp.int32, values.shape, 1) // HEAD_DIM
    zero = jnp.zeros_like(values)
    return jnp.concatenate([jnp.where(lane == h, values, zero) for h in range(4)], axis=0)


def forward_kernel(
    experts,
    x_ref,
    gain_one_ref,
    qkv_ref,
    out_w_ref,
    gain_two_ref,
    router_w_ref,
    packed_ref,
    log_ref,
    mixed_ref,
    resid_ref,
    low_two_ref,
    router_ref,
):
    images = log_ref.shape[0]
    x = x_ref[...].astype(F32)
    hat, _ = standardise(x)
    low_one = (hat * gain_one_ref[...]).astype(BF16)
    packed_ref[...] = nn(low_one, qkv_ref[...]).astype(BF16)
    for image in range(images):
        rows = slice(image * PATCHES, (image + 1) * PATCHES)
        for quad in range(2):
            cols = slice(quad * QUAD, (quad + 1) * QUAD)
            queries = packed_ref[rows, quad * QUAD : quad * QUAD + QUAD] * HEAD_DIM ** (-0.5)
            keys = packed_ref[rows, D + quad * QUAD : D + quad * QUAD + QUAD]
            values = packed_ref[rows, 2 * D + quad * QUAD : 2 * D + quad * QUAD + QUAD]
            values_t = jnp.transpose(values)
            scores = nt(head_stack(keys), queries.astype(BF16))
            parts = []
            for h in range(4):
                own = scores[h * PATCHES : (h + 1) * PATCHES]
                top = jnp.max(own, axis=0, keepdims=True)
                weights = jnp.exp(own - top)
                total = jnp.sum(weights, axis=0, keepdims=True)
                log_ref[image, quad * 4 + h : quad * 4 + h + 1, :] = top + jnp.log(total)
                part = nn(values_t[h * HEAD_DIM : (h + 1) * HEAD_DIM], weights.astype(BF16))
                parts.append(part / total)
            mixed_t = jnp.concatenate(parts, axis=0)
            mixed_ref[rows, cols] = jnp.transpose(mixed_t).astype(BF16)
    resid = x + nn(mixed_ref[...], out_w_ref[...])
    resid_ref[...] = resid
    hat_two, _ = standardise(resid)
    low_two = (hat_two * gain_two_ref[...]).astype(BF16)
    low_two_ref[...] = low_two
    logits = nn(low_two, router_w_ref[...])
    lane = lax.broadcasted_iota(jnp.int32, logits.shape, 1)
    logits = jnp.where(lane < experts, logits, -1e30)
    raised = jnp.exp(logits - jnp.max(logits, axis=1, keepdims=True))
    router_ref[...] = raised / jnp.sum(raised, axis=1, keepdims=True)


def attention_forward(x, gain_one, qkv, out_w, gain_two, router_w, experts, block):
    toks = x.shape[0]
    rows = block * PATCHES
    images = toks // PATCHES

    def tile(width):
        return pl.BlockSpec((rows, width), lambda i: (i, 0))

    return pl.pallas_call(
        partial(forward_kernel, experts),
        out_shape=(
            jax.ShapeDtypeStruct((toks, 3 * D), BF16),
            jax.ShapeDtypeStruct((images, HEADS, PATCHES), F32),
            jax.ShapeDtypeStruct((toks, D), BF16),
            jax.ShapeDtypeStruct((toks, D), F32),
            jax.ShapeDtypeStruct((toks, D), BF16),
            jax.ShapeDtypeStruct((toks, LANES), F32),
        ),
        in_specs=[
            tile(D),
            whole((1, D)),
            whole((D, 3 * D)),
            whole((D, D)),
            whole((1, D)),
            whole((D, LANES)),
        ],
        out_specs=(
            tile(3 * D),
            pl.BlockSpec((block, HEADS, PATCHES), lambda i: (i, 0, 0)),
            tile(D),
            tile(D),
            tile(D),
            tile(LANES),
        ),
        grid=(images // block,),
        compiler_params=params(),
        name="attention_forward",
        cost_estimate=pl.CostEstimate(
            flops=40_000_000_000, bytes_accessed=toks * D * 20, transcendentals=toks * 1152
        ),
    )(x, gain_one, qkv, out_w, gain_two, router_w)


GELU_C = 0.7978845608028654
GELU_A = 0.044715


def gelu_pair(v):
    square = v * v
    inner = v * (GELU_C + (GELU_C * GELU_A) * square)
    curve = jnp.tanh(inner)
    half = 0.5 + 0.5 * curve
    slope = half + 0.5 * v * (1.0 - curve * curve) * (GELU_C + (3.0 * GELU_C * GELU_A) * square)
    return v * half, slope


def expert_kernel(
    rows,
    received_ref,
    grad_ref,
    first_ref,
    second_ref,
    out_ref,
    back_ref,
    hidden_ref,
    d_pre_ref,
    d_out_ref,
    low_ref,
):
    groups = received_ref.shape[0]
    hidden_cols = first_ref.shape[2]
    for g in range(groups):
        span = slice(g * rows, (g + 1) * rows)
        gate = columns_of(received_ref[g, rows:, :], rows)
        low_ref[span] = received_ref[g, :rows]
        d_out_ref[span] = (gate * grad_ref[g].astype(F32)).astype(BF16)
    chunk = 512
    out = None
    back = None
    for start in range(0, hidden_cols, chunk):
        part = slice(start, start + chunk)
        pre = nn(low_ref[...], first_ref[0, :, part])
        act, slope = gelu_pair(pre)
        act = act.astype(BF16)
        hidden_ref[:, part] = act
        piece = nn(act, second_ref[0, part, :])
        out = piece if out is None else out + piece
        d_hidden = nt(d_out_ref[...], second_ref[0, part, :])
        d_pre = (d_hidden * slope).astype(BF16)
        d_pre_ref[:, part] = d_pre
        piece = nt(d_pre, first_ref[0, :, part])
        back = piece if back is None else back + piece
    lane = lax.broadcasted_iota(jnp.int32, (rows, LANES), 1)
    for g in range(groups):
        span = slice(g * rows, (g + 1) * rows)
        given = out[span].astype(BF16)
        out_ref[g, :rows] = given
        out_ref[g, rows:] = jnp.zeros((EXTRA, D), BF16)
        d_gate = jnp.sum(given.astype(F32) * grad_ref[g].astype(F32), axis=1, keepdims=True)
        high = d_gate.astype(BF16).astype(F32)
        wide = jnp.where(lane == 0, high, jnp.where(lane == 1, d_gate - high, 0.0))
        back_ref[g, :rows] = back[span].astype(BF16)
        back_ref[g, rows:] = rows_of(wide, rows)


def expert_apply(received, grad, first, second, block):
    groups, stride, _ = received.shape
    rows = grad.shape[1]
    wide = first.shape[2]
    total = groups * rows

    def flat(width):
        return pl.BlockSpec((block * rows, width), lambda i: (i, 0))

    return pl.pallas_call(
        partial(expert_kernel, rows),
        out_shape=(
            jax.ShapeDtypeStruct((groups, stride, D), BF16),
            jax.ShapeDtypeStruct((groups, stride, D), BF16),
            jax.ShapeDtypeStruct((total, wide), BF16),
            jax.ShapeDtypeStruct((total, wide), BF16),
            jax.ShapeDtypeStruct((total, D), BF16),
            jax.ShapeDtypeStruct((total, D), BF16),
        ),
        in_specs=[
            pl.BlockSpec((block, stride, D), lambda i: (i, 0, 0)),
            pl.BlockSpec((block, rows, D), lambda i: (i, 0, 0)),
            whole((1, D, wide)),
            whole((1, wide, D)),
        ],
        out_specs=(
            pl.BlockSpec((block, stride, D), lambda i: (i, 0, 0)),
            pl.BlockSpec((block, stride, D), lambda i: (i, 0, 0)),
            flat(wide),
            flat(wide),
            flat(D),
            flat(D),
        ),
        grid=(groups // block,),
        compiler_params=params(),
        name="expert_apply",
        cost_estimate=pl.CostEstimate(
            flops=8 * total * D * wide,
            bytes_accessed=total * wide * 4 + total * D * 12,
            transcendentals=total * wide,
        ),
    )(received, grad, first, second)


def expert_grads_kernel(low_ref, d_out_ref, hidden_ref, d_pre_ref, first_ref, second_ref):
    first_ref[0] = tn(low_ref[...], d_pre_ref[...]).astype(BF16)
    second_ref[0] = tn(hidden_ref[...], d_out_ref[...]).astype(BF16)


def expert_grads(low, d_out, hidden, d_pre):
    total, wide = hidden.shape
    chunk = 256
    return pl.pallas_call(
        expert_grads_kernel,
        out_shape=(
            jax.ShapeDtypeStruct((1, D, wide), BF16),
            jax.ShapeDtypeStruct((1, wide, D), BF16),
        ),
        in_specs=[
            whole((total, D)),
            whole((total, D)),
            pl.BlockSpec((total, chunk), lambda i: (0, i)),
            pl.BlockSpec((total, chunk), lambda i: (0, i)),
        ],
        out_specs=(
            pl.BlockSpec((1, D, chunk), lambda i: (0, 0, i)),
            pl.BlockSpec((1, chunk, D), lambda i: (0, i, 0)),
        ),
        grid=(wide // chunk,),
        compiler_params=params(),
        name="expert_grads",
        cost_estimate=pl.CostEstimate(
            flops=4 * total * D * wide, bytes_accessed=total * wide * 4, transcendentals=0
        ),
    )(low, d_out, hidden, d_pre)


def selector_cols(first, second, slots):
    slot = lax.broadcasted_iota(jnp.int32, (first.shape[0], slots), 1)
    hit = (slot == first) | (slot == second)
    return jnp.where(hit, 1.0, 0.0).astype(BF16)


def backward_kernel(
    experts,
    capacity_rows,
    flat_ref,
    returned_ref,
    cot_ref,
    resid_ref,
    router_ref,
    low_two_ref,
    mixed_ref,
    packed_ref,
    log_ref,
    x_ref,
    gain_one_ref,
    gain_two_ref,
    router_w_ref,
    out_w_ref,
    d_resid_ref,
    d_packed_ref,
    qkv_grad_ref,
    out_grad_ref,
    router_grad_ref,
    gain_two_grad_ref,
    gate_ref,
):
    step = pl.program_id(0)
    stride = capacity_rows + EXTRA
    slots = experts * stride

    @pl.when(step == 0)
    def _():
        lane = lax.broadcasted_iota(jnp.int32, (capacity_rows, LANES), 1)
        for e in range(experts):
            base = e * stride
            column = columns_of(returned_ref[base + capacity_rows : base + stride, :], capacity_rows)
            high = column.astype(BF16).astype(F32)
            wide = jnp.where(
                lane == e, high, jnp.where(lane == experts + e, column - high, 0.0)
            )
            gate_ref[base : base + capacity_rows] = wide.astype(BF16)
            gate_ref[base + capacity_rows : base + stride] = jnp.zeros((EXTRA, LANES), BF16)
        qkv_grad_ref[...] = jnp.zeros_like(qkv_grad_ref)
        out_grad_ref[...] = jnp.zeros_like(out_grad_ref)
        router_grad_ref[...] = jnp.zeros_like(router_grad_ref)
        gain_two_grad_ref[...] = jnp.zeros_like(gain_two_grad_ref)

    first, second = flat_ref[:, 0:1], flat_ref[:, 1:2]
    chosen = selector_cols(first, second, slots)
    d_two = nn(chosen, returned_ref[...])
    d_router = nn(chosen, gate_ref[...])
    d_router = d_router + pltpu.roll(d_router, LANES - experts, 1)
    router = router_ref[...]
    d_logits = router * (d_router - jnp.sum(router * d_router, axis=1, keepdims=True))
    high, low = halves(d_logits)
    d_two = d_two + nt(high, router_w_ref[...]) + nt(low, router_w_ref[...])
    low_two = low_two_ref[...]
    router_grad_ref[...] += tn(high, low_two) + tn(low, low_two)
    hat_two, inverse_two = standardise(resid_ref[...])
    gain_two_grad_ref[...] += jnp.sum(d_two * hat_two, axis=0, keepdims=True)
    d_resid = cot_ref[...] + standardise_back(hat_two, inverse_two, gain_two_ref[...], d_two)
    d_resid_ref[...] = d_resid
    d_attn = d_resid.astype(BF16)
    out_grad_ref[...] += tn(mixed_ref[...], d_attn)
    d_mixed = nt(d_attn, out_w_ref[...]).astype(BF16)
    scale = HEAD_DIM ** (-0.5)
    images = log_ref.shape[0]
    for image in range(images):
        rows = slice(image * PATCHES, (image + 1) * PATCHES)
        for quad in range(2):
            at = quad * QUAD
            queries = packed_ref[rows, at : at + QUAD] * scale
            queries = queries.astype(BF16)
            keys = packed_ref[rows, D + at : D + at + QUAD]
            values = packed_ref[rows, 2 * D + at : 2 * D + at + QUAD]
            grads = d_mixed[rows, at : at + QUAD]
            scores = nt(head_stack(keys), queries)
            d_probs = nt(head_stack(values), grads)
            keys_t = jnp.transpose(keys)
            lane = lax.broadcasted_iota(jnp.int32, (PATCHES, QUAD), 1) // HEAD_DIM
            d_values = jnp.zeros((PATCHES, QUAD), F32)
            d_keys = jnp.zeros((PATCHES, QUAD), F32)
            parts = []
            for h in range(4):
                own = slice(h * PATCHES, (h + 1) * PATCHES)
                log_row = log_ref[image, quad * 4 + h : quad * 4 + h + 1, :]
                probs = jnp.exp(scores[own] - log_row)
                d_own = d_probs[own]
                inner = jnp.sum(probs * d_own, axis=0, keepdims=True)
                d_scores = (probs * (d_own - inner)).astype(BF16)
                d_values = jnp.where(lane == h, nn(probs.astype(BF16), grads), d_values)
                d_keys = jnp.where(lane == h, nn(d_scores, queries), d_keys)
                parts.append(nn(keys_t[h * HEAD_DIM : (h + 1) * HEAD_DIM], d_scores))
            d_queries = jnp.transpose(jnp.concatenate(parts, axis=0)) * scale
            d_packed_ref[rows, at : at + QUAD] = d_queries.astype(BF16)
            d_packed_ref[rows, D + at : D + at + QUAD] = d_keys.astype(BF16)
            d_packed_ref[rows, 2 * D + at : 2 * D + at + QUAD] = d_values.astype(BF16)
    hat_one, _ = standardise(x_ref[...].astype(F32))
    low_one = (hat_one * gain_one_ref[...]).astype(BF16)
    qkv_grad_ref[...] += tn(low_one, d_packed_ref[...])


def attention_backward(
    flat,
    returned,
    cot,
    resid,
    router,
    low_two,
    mixed,
    packed,
    logs,
    x,
    gain_one,
    gain_two,
    router_w,
    out_w,
    experts,
    capacity_rows,
    block,
):
    toks = x.shape[0]
    rows = block * PATCHES
    images = toks // PATCHES
    slots = returned.shape[0]

    def tile(width):
        return pl.BlockSpec((rows, width), lambda i: (i, 0))

    return pl.pallas_call(
        partial(backward_kernel, experts, capacity_rows),
        out_shape=(
            jax.ShapeDtypeStruct((toks, D), F32),
            jax.ShapeDtypeStruct((toks, 3 * D), BF16),
            jax.ShapeDtypeStruct((D, 3 * D), F32),
            jax.ShapeDtypeStruct((D, D), F32),
            jax.ShapeDtypeStruct((LANES, D), F32),
            jax.ShapeDtypeStruct((1, D), F32),
        ),
        in_specs=[
            tile(8),
            whole((slots, D)),
            tile(D),
            tile(D),
            tile(LANES),
            tile(D),
            tile(D),
            tile(3 * D),
            pl.BlockSpec((block, HEADS, PATCHES), lambda i: (i, 0, 0)),
            tile(D),
            whole((1, D)),
            whole((1, D)),
            whole((D, LANES)),
            whole((D, D)),
        ],
        out_specs=(
            tile(D),
            tile(3 * D),
            whole((D, 3 * D)),
            whole((D, D)),
            whole((LANES, D)),
            whole((1, D)),
        ),
        grid=(images // block,),
        scratch_shapes=[pltpu.VMEM((slots, LANES), BF16)],
        compiler_params=params(),
        name="attention_backward",
        cost_estimate=pl.CostEstimate(
            flops=60_000_000_000, bytes_accessed=toks * D * 20, transcendentals=toks * 1152
        ),
    )(
        flat,
        returned,
        cot,
        resid,
        router,
        low_two,
        mixed,
        packed,
        logs,
        x,
        gain_one,
        gain_two,
        router_w,
        out_w,
    )


def input_kernel(d_packed_ref, d_resid_ref, x_ref, gain_one_ref, qkv_ref, grad_ref, gain_grad_ref):
    @pl.when(pl.program_id(0) == 0)
    def _():
        gain_grad_ref[...] = jnp.zeros_like(gain_grad_ref)

    d_one = nt(d_packed_ref[...], qkv_ref[...])
    hat, inverse = standardise(x_ref[...].astype(F32))
    gain_grad_ref[...] += jnp.sum(d_one * hat, axis=0, keepdims=True)
    grad_ref[...] = d_resid_ref[...] + standardise_back(hat, inverse, gain_one_ref[...], d_one)


def input_backward(d_packed, d_resid, x, gain_one, qkv, block):
    toks = x.shape[0]
    rows = block * PATCHES

    def tile(width):
        return pl.BlockSpec((rows, width), lambda i: (i, 0))

    return pl.pallas_call(
        input_kernel,
        out_shape=(jax.ShapeDtypeStruct((toks, D), F32), jax.ShapeDtypeStruct((1, D), F32)),
        in_specs=[tile(3 * D), tile(D), tile(D), whole((1, D)), whole((D, 3 * D))],
        out_specs=(tile(D), whole((1, D))),
        grid=(toks // rows,),
        compiler_params=params(),
        name="input_backward",
        cost_estimate=pl.CostEstimate(
            flops=2 * toks * D * 3 * D, bytes_accessed=toks * D * 20, transcendentals=0
        ),
    )(d_packed, d_resid, x, gain_one, qkv)


def combine_kernel(experts, stride, flat_ref, outputs_ref, resid_ref, router_ref, block_ref):
    first, second = flat_ref[:, 0:1], flat_ref[:, 1:2]
    lane = lax.broadcasted_iota(jnp.int32, router_ref.shape, 1) * stride
    router = router_ref[...]

    def gate(flat):
        mine = (flat >= lane) & (flat < lane + stride)
        return jnp.sum(jnp.where(mine, router, 0.0), axis=1, keepdims=True)

    slot = lax.broadcasted_iota(jnp.int32, (first.shape[0], experts * stride), 1)
    weight = jnp.where(slot == first, gate(first), jnp.where(slot == second, gate(second), 0.0))
    block_ref[...] = (resid_ref[...] + nn(weight.astype(BF16), outputs_ref[...])).astype(BF16)


def combine(flat, outputs, resid, router, experts, stride, block):
    toks = resid.shape[0]
    rows = block * PATCHES

    def tile(width):
        return pl.BlockSpec((rows, width), lambda i: (i, 0))

    return pl.pallas_call(
        partial(combine_kernel, experts, stride),
        out_shape=jax.ShapeDtypeStruct((toks, D), BF16),
        in_specs=[
            tile(8),
            whole((experts * stride, D)),
            tile(D),
            tile(LANES),
        ],
        out_specs=tile(D),
        grid=(toks // rows,),
        compiler_params=params(),
        name="combine",
        cost_estimate=pl.CostEstimate(
            flops=2 * toks * experts * stride * D, bytes_accessed=toks * D * 8, transcendentals=0
        ),
    )(flat, outputs, resid, router)


def exchange(values):
    return lax.all_to_all(values, "expert", split_axis=0, concat_axis=0, tiled=True)


def shards(
    tokens,
    gain_one,
    w_qkv,
    w_attn_out,
    gain_two,
    w_router,
    w_first,
    w_second,
    expert_ids,
    priority_ranks,
    cotangent,
):
    tok_rows = tokens.shape[0]
    experts = w_router.shape[1]
    capacity = max(2, tok_rows // experts)
    capacity_rows = -(-capacity // 16) * 16
    stride = capacity_rows + EXTRA
    gain_one = gain_one.reshape(1, D)
    gain_two = gain_two.reshape(1, D)
    router_w = jnp.pad(w_router, ((0, 0), (0, LANES - experts)))

    flat, flat_cols = route(expert_ids.T, priority_ranks, experts, capacity, stride)
    grad_rows = exchange(dispatch_grad(flat, cotangent, experts, capacity_rows, stride))
    packed, logs, mixed, resid, low_two, router = attention_forward(
        tokens, gain_one, w_qkv, w_attn_out, gain_two, router_w, experts, 2
    )
    received = exchange(dispatch(flat, low_two, router, experts, capacity_rows, stride))
    outputs, back, hidden, d_pre, d_out, low = expert_apply(
        received, grad_rows, w_first, w_second, 2
    )
    returned = exchange(back).reshape(experts * stride, D)
    outputs = exchange(outputs).reshape(experts * stride, D)
    first_grad, second_grad = expert_grads(low, d_out, hidden, d_pre)
    first_grad = lax.psum(first_grad, "dp").astype(F32)
    second_grad = lax.psum(second_grad, "dp").astype(F32)
    d_resid, d_packed, qkv_grad, out_grad, router_grad, gain_two_grad = attention_backward(
        flat_cols,
        returned,
        cotangent,
        resid,
        router,
        low_two,
        mixed,
        packed,
        logs,
        tokens,
        gain_one,
        gain_two,
        router_w,
        w_attn_out,
        experts,
        capacity_rows,
        2,
    )
    grad_tokens, gain_one_grad = input_backward(d_packed, d_resid, tokens, gain_one, w_qkv, 4)
    block_out = combine(flat_cols, outputs, resid, router, experts, stride, 4)
    router_grad = router_grad[:experts].T
    summed = lax.psum(
        (qkv_grad, out_grad, router_grad, gain_one_grad, gain_two_grad), ("dp", "expert")
    )
    return (
        block_out,
        grad_tokens,
        summed[3].reshape(D),
        summed[0],
        summed[1],
        summed[4].reshape(D),
        summed[2],
        first_grad,
        second_grad,
    )


def solution(mesh):
    both = P(("dp", "expert"), None)
    expert = P("expert", None, None)
    in_specs = (both, P(), P(), P(), P(), P(), expert, expert, both, both, both)
    out_specs = (both, both, P(), P(), P(), P(), P(), expert, expert)
    return jax.shard_map(shards, mesh=mesh, in_specs=in_specs, out_specs=out_specs, check_vma=False)
```

time: 848 us -> 464 us (0.55)
  local copies, waits for them, and re-layouts: 260 us -> 9.37 us
  matrix products: 238 us -> 0 us
  Pallas kernels: 0 us -> 190 us
  other arithmetic: 109 us -> 6.89 us
  blocking collectives: 38.7 us -> 103 us
  waiting for transfers between devices: 160 us -> 126 us
    dot_general x26 -> x0, matrix products: 238 us -> none  [the longest x1 22 us: shards(): jnp.einsum('erd,edf->erf', received, w_first, preferred_element_type=jnp....]
    pallas_call x0 -> x9, Pallas kernels: none -> 190 us  [the longest x1 61.4 us: attention_backward(): pl.pallas_call(partial(backward_kernel, experts, capacity_rows), out_shap...]
    unnamed x124 -> x17, local copies, waits for them, and re-layouts: 87.4 us -> 7.96 us
    convert_element_type x5 -> x0, local copies, waits for them, and re-layouts: 75.3 us -> none  [the longest x1 21.1 us: shards(): d_packed = jnp.stack([d_queries, d_keys, d_values], axis=2).reshape(tok_r...]
    all_to_all x0 -> x1, blocking collectives: none -> 61.9 us  [exchange(): lax.all_to_all(values, 'expert', split_axis=0, concat_axis=0, tiled=True)]
    all_to_all x4 -> x3, waiting for transfers between devices: 93 us -> 52.1 us  [exchange(): lax.all_to_all(values, 'expert', split_axis=0, concat_axis=0, tiled=True)]
    unnamed x6 -> x0, other arithmetic: 35.2 us -> none
    reshape x3 -> x0, local copies, waits for them, and re-layouts: 32.9 us -> none  [the longest x1 18 us: shards(): grouped = packed.reshape(images, PATCHES, 3, HEADS, HEAD_DIM)]
  transfers between devices with their start and end apart: 6 -> 5, of which waited for: 5 -> 3; matrix products, arithmetic and copies ran while one was open for 40% -> 2% of each run, Pallas kernels for 0% -> 31%
where the time goes in v1:
time: 464 us; the launch traced here: 463 us
  Pallas kernels  190 us (41%)
  waiting for transfers between devices  126 us (27%)
  blocking collectives  103 us (22%)
  between operations  14.1 us (3%)
  starting transfers between devices  14 us (3%)
  local copies, waits for them, and re-layouts  9.37 us (2%)
  other arithmetic  6.89 us (1%)
    psum x1, waiting for transfers between devices, shards(): lax.psum((qkv_grad, out_grad, router_grad, gain_one_grad, gain_two_grad),...  73.4 us
    all_to_all x1, blocking collectives, exchange(): lax.all_to_all(values, 'expert', split_axis=0, concat_axis=0, tiled=True)  61.9 us
    pallas_call x1, Pallas kernels, attention_backward(): pl.pallas_call(partial(backward_kernel, experts, capacity_rows), out_shap...  61.4 us
    all_to_all x3, waiting for transfers between devices, exchange(): lax.all_to_all(values, 'expert', split_axis=0, concat_axis=0, tiled=True)  52.1 us
    psum x1, blocking collectives, shards(): lax.psum((qkv_grad, out_grad, router_grad, gain_one_grad, gain_two_grad),...  41 us
    pallas_call x1, Pallas kernels, expert_apply(): pl.pallas_call(partial(expert_kernel, rows), out_shape=(jax.ShapeDtypeStr...  30.9 us
    pallas_call x1, Pallas kernels, attention_forward(): pl.pallas_call(partial(forward_kernel, experts), out_shape=(jax.ShapeDtyp...  27.1 us
    pallas_call x1, Pallas kernels, expert_grads(): pl.pallas_call(expert_grads_kernel, out_shape=(jax.ShapeDtypeStruct((1, D...  17 us
  transfers between devices with their start and end apart: 5, of which 3 were waited for; matrix products, arithmetic and copies ran while one was open for 2% of the time, Pallas kernels for 31%

profile of v1, /device:TPU:0, one launch (start us, length us, event | category | flops | bytes accessed | tf_op | source)
XLA Modules:
  0.0 463.1 jit_solution(13299625179186824462)
XLA Ops:
  7.2 4.1 route.1
  11.3 10.3 %dispatch_grad.1 = bf16[8,288,512]{2,1,0:T(8,128)(2,1)} custom-call(s32[8,2304]{1,0:T(8,128)} %get-tuple-element.34.flat_ref, f32[2304,512]{1,0:T(8,128)} %cot_ref.1), custom_call_target="tpu_custom_call" | custom-call | flops 5435817984 | bytes 7077888 | tf_op jit(solution)/shard_map/dispatch_grad/pallas_call | solution.py:131
  21.6 6.5 %all-to-all-start.1 = ((bf16[8,288,512]{2,1,0:T(8,128)(2,1)}), bf16[8,288,512]{2,1,0:T(8,128)(2,1)S(1)}, u32[]{:S(2)}, u32[]{:S(2)}) async-start(bf16[8,288,512]{2,1,0:T(8,128)(2,1)} %dispatch_grad.1), calls=%async_computation.1 | async-start | bytes 4718592 | tf_op jit(solution)/shard_map/all_to_all | solution.py:703
  28.1 0.2 copy.20
  28.2 0.7 pad.4.router_w_ref
  28.9 27.1 %attention_forward.1 = (bf16[2304,1536]{1,0:T(8,128)(2,1)}, f32[16,8,144]{2,1,0:T(8,128)}, bf16[2304,512]{1,0:T(8,128)(2,1)}, f32[2304,512]{1,0:T(8,128)}, bf16[...) custom-call(bf16[2304,512]{1,0:T(8,128)(2,1)} %x_ref.5, f32[1,512]{1,0:T(1,128)} %bitcast.11, bf16[512,1536]{1,0:T(8,128)(2,1)} %qkv_ref.3, ...), custom_call_target="tpu_custom_call" | custom-call | flops 40000000000 | bytes 23592960 | tf_op jit(solution)/shard_map/attention_forward/pallas_call | solution.py:263
  56.0 14.9 %dispatch.1 = bf16[8,304,512]{2,1,0:T(8,128)(2,1)} custom-call(s32[8,2304]{1,0:T(8,128)} %get-tuple-element.34.flat_ref, bf16[2304,512]{1,0:T(8,128)(2,1)} %get-tuple-element.35.low_ref.low_two_ref, f32[2304,128]{1,0:T(8,128)} %get-tuple-element.36.router_ref), custom_call_target="tpu_custom_call" | custom-call | flops 8153726976 | bytes 7077888 | tf_op jit(solution)/shard_map/dispatch/pallas_call | solution.py:180
  71.0 11.8 %all-to-all-done.1.grad_ref = bf16[8,288,512]{2,1,0:T(8,128)(2,1)S(1)} async-done(((bf16[8,288,512]{2,1,0:T(8,128)(2,1)}), bf16[8,288,512]{2,1,0:T(8,128)(2,1)S(1)}, u32[]{:S(2)}, u32[]{:S(2)}) %all-to-all-start.1) | async-done | bytes 2359328 | tf_op jit(solution)/shard_map/all_to_all | solution.py:703
  82.7 61.9 %all_to_all.20.received_ref = bf16[8,304,512]{2,1,0:T(8,128)(2,1)} all-to-all(bf16[8,304,512]{2,1,0:T(8,128)(2,1)} %dispatch.1), channel_id=1, replica_groups=mesh['dp'=4,'expert'=8] {'expert'}, dimensions={0} | all-to-all | bytes 4980736 | tf_op jit(solution)/shard_map/all_to_all | solution.py:703
  144.6 30.9 %expert_apply.1 = (bf16[8,304,512]{2,1,0:T(8,128)(2,1)}, bf16[8,304,512]{2,1,0:T(8,128)(2,1)}, bf16[2304,2048]{1,0:T(8,128)(2,1)}, bf16[2304,2048]{1,0:T(8,128)(...) custom-call(bf16[8,304,512]{2,1,0:T(8,128)(2,1)} %all_to_all.20.received_ref, bf16[8,288,512]{2,1,0:T(8,128)(2,1)} %copy-done.2, ...), custom_call_target="tpu_custom_call" | custom-call | flops 19327352832 | bytes 33030144 | tf_op jit(solution)/shard_map/expert_apply/pallas_call | solution.py:369
  175.5 3.6 all-to-all-start.3
  179.1 0.0 all-reduce.9.cloned.1.call-start
  179.2 17.0 %expert_grads.1 = (bf16[1,512,2048]{2,1,0:T(8,128)(2,1)}, bf16[1,2048,512]{2,1,0:T(8,128)(2,1)}) custom-call(bf16[2304,512]{1,0:T(8,128)(2,1)} %get-tuple-element.51.low_ref, bf16[2304,512]{1,0:T(8,128)(2,1)} %get-tuple-element.52.d_out_ref, bf16[2304,2048]{1,0:T(8,128)(2,1)} %get-tuple-element.53.hidden_ref, bf16[2304,2048]{1,0:T(8,128)(2,1)} %get-tuple-element.54.d_pre_ref), custom_call_target="tpu_custom_call" | custom-call | flops 9663676416 | bytes 18874368 | tf_op jit(solution)/shard_map/expert_grads/pallas_call | solution.py:412
  196.2 0.0 all-reduce.9.cloned.1.call-update
  196.2 40.3 %all-to-all-done.3 = bf16[8,304,512]{2,1,0:T(8,128)(2,1)S(1)} async-done(((bf16[8,304,512]{2,1,0:T(8,128)(2,1)}), bf16[8,304,512]{2,1,0:T(8,128)(2,1)S(1)}, u32[]{:S(2)}, u32[]{:S(2)}) %all-to-all-start.3) | async-done | bytes 2490400 | tf_op jit(solution)/shard_map/all_to_all | solution.py:703
  236.5 1.4 copy-done.1
  238.0 3.6 all-to-all-start.2
  241.6 0.3 all-reduce.7.cloned.1.call-start
  241.9 61.4 %attention_backward.1 = (f32[2304,512]{1,0:T(8,128)}, bf16[2304,1536]{1,0:T(8,128)(2,1)}, f32[512,1536]{1,0:T(8,128)}, f32[512,512]{1,0:T(8,128)}, f32[128,512]{1,0:T(8,128)}, /*index=5*/f32[1,512]{1,0:T(1,128)}) custom-call(s32[2304,8]{1,0:T(8,128)} %get-tuple-element.33.flat_ref, bf16[2432,512]{1,0:T(8,128)(2,1)} %bitcast.10, f32[2304,512]{1,0:T(8,128)} %cot_ref.1, ...), custom_call_target="tpu_custom_call" | custom-call | flops 60000002048 | bytes 23592960 | tf_op jit(solution)/shard_map/attention_backward/pallas_call | solution.py:571
  303.3 0.0 all-reduce.7.cloned.1.call-update
  303.3 0.0 all-reduce.9.cloned.1.call-done
  303.4 4.3 convert_element_type.8
  307.6 2.6 convert_element_type.9
  310.2 0.7 slice_bitcast_fusion
  311.0 11.0 %input_backward.1 = (f32[2304,512]{1,0:T(8,128)}, f32[1,512]{1,0:T(1,128)}) custom-call(bf16[2304,1536]{1,0:T(8,128)(2,1)} %get-tuple-element.43.d_packed_ref, f32[2304,512]{1,0:T(8,128)} %get-tuple-element.44.d_resid_ref, bf16[2304,512]{1,0:T(8,128)(2,1)} %x_ref.5, f32[1,512]{1,0:T(1,128)} %bitcast.13, bf16[512,1536]{1,0:T(8,128)(2,1)} %qkv_ref.3), custom_call_target="tpu_custom_call" | custom-call | flops 3623878656 | bytes 23592960 | tf_op jit(solution)/shard_map/input_backward/pallas_call | solution.py:648
  322.0 41.0 %all-reduce.1 = (f32[512]{0:T(512)}, f32[512]{0:T(512)}, f32[512,8]{0,1:T(8,128)}) all-reduce(f32[512]{0:T(512)} %bitcast.15, f32[512]{0:T(512)S(1)} %bitcast.14, f32[512,8]{0,1:T(8,128)S(1)} %slice_bitcast_fusion), channel_id=1, replica_groups=mesh['dp'=4,'expert'=8] {'dp','expert'}, use_global_device_ids=true, to_apply=%region_0.1 | all-reduce | flops 5120 | bytes 40960 | tf_op jit(solution)/shard_map/psum | solution.py:764
  363.0 0.0 all-to-all-done.2
  363.0 1.5 copy-done
  364.5 13.5 %combine.1 = bf16[2304,512]{1,0:T(8,128)(2,1)} custom-call(s32[2304,8]{1,0:T(8,128)} %get-tuple-element.33.flat_ref, bf16[2432,512]{1,0:T(8,128)(2,1)} %bitcast.9, f32[2304,512]{1,0:T(8,128)} %get-tuple-element.38.resid_ref, f32[2304,128]{1,0:T(8,128)} %get-tuple-element.36.router_ref), custom_call_target="tpu_custom_call" | custom-call | flops 5737807872 | bytes 9437184 | tf_op jit(solution)/shard_map/combine/pallas_call | solution.py:683
  378.1 73.4 %all-reduce.7.cloned.1.call-done = (f32[512,1536]{1,0:T(8,128)}, f32[512,512]{1,0:T(8,128)}) async-done(((f32[512,1536]{1,0:T(8,128)}, f32[512,512]{1,0:T(8,128)}), (f32[512,1536]{1,0:T(8,128)}, f32[512,512]{1,0:T(8,128)})) %all-reduce.7.cloned.1.call-update) | async-done | bytes 4194320 | tf_op jit(solution)/shard_map/psum | solution.py:764
  451.4 3.8 copy.25
  455.3 1.0 copy.26
  (12 shorter events, 0.0 us)
Async XLA Ops:
  21.6 6.5 %copy-start.5 = (bf16[512,8]{0,1:T(8,128)(2,1)S(1)}, bf16[512,8]{0,1:T(8,128)(2,1)}, u32[]{:S(2)}) copy-start(bf16[512,8]{0,1:T(8,128)(2,1)} %param.16) | copy-start | bytes 24580
  21.6 61.1 %all-to-all-start.1 = ((bf16[8,288,512]{2,1,0:T(8,128)(2,1)}), bf16[8,288,512]{2,1,0:T(8,128)(2,1)S(1)}, u32[]{:S(2)}, u32[]{:S(2)}) async-start(bf16[8,288,512]{2,1,0:T(8,128)(2,1)} %dispatch_grad.1), calls=%async_computation.1 | async-start | bytes 4718592 | tf_op jit(solution)/shard_map/all_to_all | solution.py:703
  82.7 61.9 %copy-start.2 = (bf16[8,288,512]{2,1,0:T(8,128)(2,1)}, bf16[8,288,512]{2,1,0:T(8,128)(2,1)S(1)}, u32[]{:S(2)}) copy-start(bf16[8,288,512]{2,1,0:T(8,128)(2,1)S(1)} %all-to-all-done.1.grad_ref) | copy-start | bytes 7077892
  175.5 61.1 %all-to-all-start.3 = ((bf16[8,304,512]{2,1,0:T(8,128)(2,1)}), bf16[8,304,512]{2,1,0:T(8,128)(2,1)S(1)}, u32[]{:S(2)}, u32[]{:S(2)}) async-start(bf16[8,304,512]{2,1,0:T(8,128)(2,1)} %get-tuple-element.39), calls=%async_computation.3 | async-start | bytes 4980736 | tf_op jit(solution)/shard_map/all_to_all | solution.py:703
  179.1 124.2 %all-reduce.9.cloned.1.call-start = ((), (), s32[]{:S(2)}) async-start(), calls=%async_computation.5 | async-start | bytes 8388608 | tf_op jit(solution)/shard_map/psum | solution.py:740
  236.5 1.4 copy-start.1
  238.0 125.0 %all-to-all-start.2 = ((bf16[8,304,512]{2,1,0:T(8,128)(2,1)}), bf16[8,304,512]{2,1,0:T(8,128)(2,1)S(1)}, u32[]{:S(2)}, u32[]{:S(2)}) async-start(bf16[8,304,512]{2,1,0:T(8,128)(2,1)} %get-tuple-element.37), calls=%async_computation.2 | async-start | bytes 4980736 | tf_op jit(solution)/shard_map/all_to_all | solution.py:703
  241.6 209.8 %all-reduce.7.cloned.1.call-start = ((), (), s32[]{:S(2)}) async-start(), calls=%async_computation.4 | async-start | bytes 8388608 | tf_op jit(solution)/shard_map/psum | solution.py:764
  303.3 4.3 copy-start.3
  311.0 11.0 %copy-start.6 = (f32[1,512]{1,0:T(1,128)S(1)}, f32[1,512]{1,0:T(1,128)}, u32[]{:S(2)}) copy-start(f32[1,512]{1,0:T(1,128)} %get-tuple-element.49) | copy-start | bytes 6148
  363.0 1.5 copy-start
  451.4 3.8 copy-start.4
Sparse Core Ops, SparseCore 0:
  196.3 105.5 all-reduce.8
  309.1 142.2 all-reduce.6
